TPU v7x, 32 devices: a whole 2x2x4 slice. The times are simulated.
32 devices in a mesh: grp: 8 (over y, x, core), tp: 4 (over z).
Axes of the slice: x: 2, y: 2, z: 4, core: 2. Of those that a mesh axis runs over, the one named last changes fastest.
Arguments:
- queries: bfloat16 [32, 2, 4096], P('grp'), may hold values from -8 to 8
- cache_keys: bfloat16 [32, 512, 512], P('grp', 'tp'), may hold values from -8 to 8
- cache_values: bfloat16 [32, 512, 512], P('grp', 'tp'), may hold values from -6 to 6
- new_keys: bfloat16 [32, 2, 512], P('grp'), may hold values from -6 to 6
- new_values: bfloat16 [32, 2, 512], P('grp'), may hold values from -6 to 6
- lengths: int32 [32], P('grp'), may hold values from 2 to 512
- residual: bfloat16 [32, 2, 4096], P('grp'), may hold values from -0.1796875 to 0.1796875
- norm_gain: float32 [4096], replicated, may hold values from 0.25 to 1.75
- w_gate: float32 [4096, 2400], P('grp', 'tp'), may hold values from -0.09375 to 0.09375
- w_down: float32 [4096, 2400], P('grp', 'tp'), may hold values from -0.125 to 0.125
Outputs:
- mixed: bfloat16 [32, 2, 4096], P('grp')
All inputs are finite; a program needn't handle non-finite values.
Results may differ from a plain program's by a relative error of at most 0.028.
Values may be sent and summed in bfloat16 or wider, within the bound.
A program may use at most 64 MiB of HBM per device.

v0:
```python
import jax
import jax.numpy as jnp
from jax import lax
from jax.sharding import PartitionSpec as P

HD = 128
KVH = 4


masked_score = -1e30


def merged_2(shard, axis, join):
    gathered = jax.tree.map(
        lambda a, kind: lax.all_gather(a.astype(kind), axis),
        shard,
        jax.tree.map(lambda a: jnp.bfloat16 if a.dtype == jnp.float32 else a.dtype, shard),
    )

    def take(source):
        return jax.tree.map(
            lambda a, own: lax.dynamic_index_in_dim(a, source, 0, False).astype(own.dtype),
            gathered,
            shard,
        )

    return lax.fori_loop(
        1, lax.axis_size(axis), lambda source, state: join(state, take(source)), take(0)
    )


def combine_parts(earlier, later):
    first_max, first_total, first_accum = earlier
    second_max, second_total, second_accum = later
    joint_max = jnp.maximum(first_max, second_max)
    first_factor = jnp.exp(first_max - joint_max)
    second_factor = jnp.exp(second_max - joint_max)
    joint_total = first_total * first_factor + second_total * second_factor
    joint_accum = first_accum * first_factor[..., None] + second_accum * second_factor[..., None]
    return (joint_max, joint_total, joint_accum)


def partial_softmax(scores, visible, value_heads, formula):
    scores = jnp.where(visible, scores, masked_score)
    highest = jnp.max(scores, axis=-1)
    weights = jnp.where(visible, jnp.exp(scores - highest[..., None]), 0.0)
    totals = jnp.sum(weights, axis=-1)
    accum = jnp.einsum(
        formula, weights.astype(jnp.bfloat16), value_heads, preferred_element_type=jnp.float32
    )
    return (highest, totals, accum)


def shards(
    queries,
    cache_keys,
    cache_values,
    new_keys,
    new_values,
    lengths,
    residual,
    norm_gain,
    w_gate,
    w_down,
):
    row_count, step_count, features = queries.shape
    positions = cache_keys.shape[1]
    per_group = features // (KVH * HD)
    inv_root = HD ** (-0.5)
    query_heads = queries.reshape(row_count, step_count, KVH, per_group, HD)
    key_heads = cache_keys.reshape(row_count, positions, KVH, HD)
    value_heads = cache_values.reshape(row_count, positions, KVH, HD)
    cached_scores = (
        jnp.einsum("rsjgd,rcjd->rsjgc", query_heads, key_heads, preferred_element_type=jnp.float32)
        * inv_root
    )
    offset = lax.axis_index("tp") * positions
    places = offset + lax.broadcasted_iota(jnp.int32, (row_count, positions), 1)
    visible = (places < lengths[:, None])[:, None, None, None, :]
    local_part = partial_softmax(cached_scores, visible, value_heads, "rsjgc,rcjd->rsjgd")
    merged = merged_2(local_part, "tp", combine_parts)
    fresh_key_heads = new_keys.reshape(row_count, step_count, KVH, HD)
    fresh_value_heads = new_values.reshape(row_count, step_count, KVH, HD)
    fresh_scores = (
        jnp.einsum(
            "rsjgd,rtjd->rsjgt", query_heads, fresh_key_heads, preferred_element_type=jnp.float32
        )
        * inv_root
    )
    causal = lax.broadcasted_iota(jnp.int32, (step_count, step_count), 0) >= lax.broadcasted_iota(
        jnp.int32, (step_count, step_count), 1
    )
    causal = causal[None, :, None, None, :]
    fresh_part = partial_softmax(fresh_scores, causal, fresh_value_heads, "rsjgt,rtjd->rsjgd")
    joint_max, joint_total, joint_accum = combine_parts(merged, fresh_part)
    context = (joint_accum / joint_total[..., None]).reshape(row_count, step_count, features)
    summed = residual.astype(jnp.float32) + context
    mean_square = jnp.mean(summed * summed, axis=-1, keepdims=True)
    normed = (summed * lax.rsqrt(mean_square + 1e-05) * norm_gain).astype(jnp.bfloat16)
    flat = normed.reshape(row_count * step_count, features)
    gate_policy, down_policy = (
        lax.all_gather(w_gate.astype(jnp.bfloat16), "grp", axis=0, tiled=True),
        lax.all_gather(w_down.astype(jnp.bfloat16), "grp", axis=0, tiled=True),
    )
    gate = jnp.dot(flat, gate_policy, preferred_element_type=jnp.float32)
    hidden = jax.nn.silu(gate).astype(jnp.bfloat16)
    partial_sum = lax.dot_general(
        hidden, down_policy, (((1,), (1,)), ((), ())), preferred_element_type=jnp.float32
    )
    mlp = lax.psum(partial_sum.astype(jnp.bfloat16), "tp").astype(jnp.float32)
    return (summed + mlp.reshape(row_count, step_count, features)).astype(jnp.bfloat16)


def solution(mesh):
    return jax.shard_map(
        shards,
        mesh=mesh,
        in_specs=(
            P("grp", None, None),
            P("grp", "tp", None),
            P("grp", "tp", None),
            P("grp", None, None),
            P("grp", None, None),
            P("grp"),
            P("grp", None, None),
            P(),
            P("grp", "tp"),
            P("grp", "tp"),
        ),
        out_specs=P("grp", None, None),
        check_vma=False,
    )
```

profile of v0, /device:TPU:0, one launch (start us, length us, event | category | flops | bytes accessed | tf_op | source)
XLA Modules:
  0.0 144.4 jit_solution(1992973439651698858)
XLA Ops:
  6.5 0.0 copy-start
  6.5 0.0 copy-start.4
  6.5 0.0 copy-start.2
  6.5 0.0 copy-start.7
  6.5 0.0 copy-start.3
  6.5 0.0 copy-start.6
  6.6 0.0 all-gather.6.cloned.1.call-start
  6.6 2.3 %convert_element_type.133 = bf16[512,600]{0,1:T(8,128)(2,1)} convert(f32[512,600]{0,1:T(8,128)} %param.20) | non-fusion elementwise | flops 307200 | bytes 1843200 | tf_op jit(solution)/shard_map/convert_element_type | solution.py:102
  8.9 0.0 all-gather.6.cloned.1.call-update
  8.9 0.0 all-gather.8.cloned.1.call-start
  8.9 2.2 %convert_element_type.135 = bf16[512,600]{0,1:T(8,128)(2,1)} convert(f32[512,600]{0,1:T(8,128)} %param.21) | non-fusion elementwise | flops 307200 | bytes 1843200 | tf_op jit(solution)/shard_map/convert_element_type | solution.py:103
  11.2 0.0 all-gather.8.cloned.1.call-update
  11.2 0.0 all-reduce.2.cloned.1.call-start
  11.2 0.0 copy-done.4
  11.2 0.1 reshape.100
  11.3 0.0 copy-done.2
  11.3 0.1 reshape.99
  11.5 0.0 copy-done.7
  11.5 0.1 broadcast_compare_fusion
  11.5 0.5 fusion.35
  12.0 0.0 copy-start.1
  12.0 0.2 fusion.14
  12.3 0.0 copy-done.3
  12.3 0.0 copy-start.5
  12.3 0.1 reshape.101
  12.4 0.3 fusion.8
  12.8 14.8 %all-gather = bf16[16,2,4,8]{3,2,1,0:T(4,128)(2,1)S(1)} all-gather(bf16[4,2,4,8]{3,2,1,0:T(4,128)(2,1)S(1)} %copy.56), channel_id=2, replica_groups=mesh['grp'=8,'tp'=4] {'tp'}, dimensions={0}, use_global_device_ids=true | all-gather | bytes 2560 | tf_op jit(solution)/shard_map/all_gather | solution.py:15
  27.6 13.1 %all-gather.1 = bf16[16,2,4,8]{3,2,1,0:T(4,128)(2,1)S(1)} all-gather(bf16[4,2,4,8]{3,2,1,0:T(4,128)(2,1)S(1)} %copy.57), channel_id=3, replica_groups=mesh['grp'=8,'tp'=4] {'tp'}, dimensions={0}, use_global_device_ids=true | all-gather | bytes 2560 | tf_op jit(solution)/shard_map/all_gather | solution.py:15
  40.7 13.8 %all-gather.2 = bf16[16,2,4,8,128]{4,3,2,1,0:T(8,128)(2,1)S(1)} all-gather(bf16[4,2,4,8,128]{4,3,2,1,0:T(8,128)(2,1)S(1)} %copy.59), channel_id=4, replica_groups=mesh['grp'=8,'tp'=4] {'tp'}, dimensions={0}, use_global_device_ids=true | all-gather | bytes 327680 | tf_op jit(solution)/shard_map/all_gather | solution.py:15
  54.5 0.0 copy-done.6
  54.5 0.4 fusion.36
  54.9 0.1 fusion.28
  55.1 0.7 while.19
  55.2 0.2 fusion.45
  55.4 0.2 fusion.45
  55.6 0.2 fusion.45
  55.9 0.0 copy-done
  55.9 0.3 fusion.7
  56.2 0.1 reshape.104
  56.3 0.0 copy-done.1
  56.3 0.2 multiply_reduce_fusion
  56.5 0.0 copy-done.5
  56.5 0.1 multiply_convert_fusion
  56.7 0.0 all-gather.6.cloned.1.call-done
  56.7 38.4 %all-gather.8.cloned.1.call-done = bf16[4096,600]{0,1:T(8,128)(2,1)} async-done(((bf16[512,600]{0,1:T(8,128)(2,1)}), bf16[4096,600]{0,1:T(8,128)(2,1)}) %all-gather.8.cloned.1.call-update) | async-done | bytes 4915216 | tf_op jit(solution)/shard_map/all_gather | solution.py:103
  95.1 6.3 %convolution_convert_fusion = bf16[8,4096]{1,0:T(8,128)(2,1)S(1)} fusion(bf16[4096,600]{0,1:T(8,128)(2,1)} %all-gather.8.cloned.1.call-done, bf16[8,4096]{1,0:T(8,128)(2,1)S(1)} %reshape.105, bf16[4096,600]{0,1:T(8,128)(2,1)} %all-gather.6.cloned.1.call-done), kind=kOutput, calls=%fused_computation.8 | convolution fusion | flops 78699968 | bytes 9961472 | tf_op jit(solution)/shard_map/dot_general | solution.py:107
  101.4 0.7 reshape.106
  102.1 0.0 all-reduce.2.cloned.1.call-update
  102.1 34.1 %all-reduce.2.cloned.1.call-done = bf16[4,2,4096]{2,1,0:T(2,128)(2,1)} async-done(((bf16[4,2,4096]{2,1,0:T(2,128)(2,1)}), bf16[4,2,4096]{2,1,0:T(2,128)(2,1)}) %all-reduce.2.cloned.1.call-update) | async-done | bytes 65552 | tf_op jit(solution)/shard_map/psum | solution.py:110
  136.3 1.6 %add_convert_fusion = bf16[4,2,4096]{2,1,0:T(2,128)(2,1)} fusion(bf16[4,2,4096]{2,1,0:T(2,128)(2,1)} %all-reduce.2.cloned.1.call-done, f32[4,2,4096]{2,1,0:T(2,128)S(1)} %reshape.104, bf16[4,2,4096]{2,1,0:T(2,128)(2,1)S(1)} %copy-done.1), kind=kLoop, calls=%fused_computation.24 | loop fusion | flops 163840 | bytes 327680 | tf_op jit(solution)/shard_map/convert_element_type | solution.py:111
  (19 shorter events, 0.3 us)
Async XLA Ops:
  6.5 49.4 %copy-start = (bf16[4,2,512]{2,1,0:T(2,128)(2,1)S(1)}, bf16[4,2,512]{2,1,0:T(2,128)(2,1)}, u32[]{:S(2)}) copy-start(bf16[4,2,512]{2,1,0:T(2,128)(2,1)} %param.16) | copy-start | bytes 24580
  6.5 4.7 %copy-start.4 = (bf16[4,2,4096]{2,1,0:T(2,128)(2,1)S(1)}, bf16[4,2,4096]{2,1,0:T(2,128)(2,1)}, u32[]{:S(2)}) copy-start(bf16[4,2,4096]{2,1,0:T(2,128)(2,1)} %param.12) | copy-start | bytes 196612
  6.5 4.8 %copy-start.2 = (bf16[4,128,512]{2,1,0:T(8,128)(2,1)S(1)}, bf16[4,128,512]{2,1,0:T(8,128)(2,1)}, u32[]{:S(2)}) copy-start(bf16[4,128,512]{2,1,0:T(8,128)(2,1)} %param.13) | copy-start | bytes 1572868
  6.5 4.9 %copy-start.7 = (s32[4]{0:T(128)S(1)}, s32[4]{0:T(128)}, u32[]{:S(2)}) copy-start(s32[4]{0:T(128)} %param.17) | copy-start | bytes 52
  6.5 5.7 %copy-start.3 = (bf16[4,128,512]{2,1,0:T(8,128)(2,1)S(1)}, bf16[4,128,512]{2,1,0:T(8,128)(2,1)}, u32[]{:S(2)}) copy-start(bf16[4,128,512]{2,1,0:T(8,128)(2,1)} %param.14) | copy-start | bytes 1572868
  6.5 48.0 %copy-start.6 = (bf16[4,2,512]{2,1,0:T(2,128)(2,1)S(1)}, bf16[4,2,512]{2,1,0:T(2,128)(2,1)}, u32[]{:S(2)}) copy-start(bf16[4,2,512]{2,1,0:T(2,128)(2,1)} %param.15) | copy-start | bytes 24580
  6.6 50.1 %all-gather.6.cloned.1.call-start = ((), (), s32[]{:S(2)}) async-start(), calls=%async_computation | async-start | bytes 5529600 | tf_op jit(solution)/shard_map/all_gather | solution.py:102
  8.9 86.2 %all-gather.8.cloned.1.call-start = ((), (), s32[]{:S(2)}) async-start(), calls=%async_computation.1 | async-start | bytes 5529600 | tf_op jit(solution)/shard_map/all_gather | solution.py:103
  11.2 125.1 %all-reduce.2.cloned.1.call-start = ((), (), s32[]{:S(2)}) async-start(), calls=%async_computation.2 | async-start | bytes 131072 | tf_op jit(solution)/shard_map/psum | solution.py:110
  12.0 44.3 %copy-start.1 = (bf16[4,2,4096]{2,1,0:T(2,128)(2,1)S(1)}, bf16[4,2,4096]{2,1,0:T(2,128)(2,1)}, u32[]{:S(2)}) copy-start(bf16[4,2,4096]{2,1,0:T(2,128)(2,1)} %param.18) | copy-start | bytes 196612
  12.3 44.2 %copy-start.5 = (f32[4096]{0:T(1024)S(1)}, f32[4096]{0:T(1024)}, u32[]{:S(2)}) copy-start(f32[4096]{0:T(1024)} %param.19) | copy-start | bytes 49156
Sparse Core Ops, SparseCore 0:
  9.3 43.2 all-gather.5
  54.5 40.5 all-gather.7
  102.3 33.9 all-reduce.1
where the time goes:
time: 145 us; the launch traced here: 144 us
  waiting for transfers between devices  72.6 us (50%)
  blocking collectives  41.7 us (29%)
  between operations  13.4 us (9%)
  matrix products  7.78 us (5%)
  other arithmetic  7.49 us (5%)
    all_gather x3, blocking collectives, merged_2(): lax.all_gather(a.astype(kind), axis)  41.7 us
    all_gather x1, waiting for transfers between devices, shards(): lax.all_gather(w_down.astype(jnp.bfloat16), 'grp', axis=0, tiled=True)  38.4 us
    psum x1, waiting for transfers between devices, shards(): mlp = lax.psum(partial_sum.astype(jnp.bfloat16), 'tp').astype(jnp.float32)  34.1 us
    dot_general x1, matrix products, shards(): lax.dot_general(hidden, down_policy, (((1,), (1,)), ((), ())), preferred_...  6.29 us
  transfers between devices with their start and end apart: 3, of which 2 were waited for; matrix products, arithmetic and copies ran while one was open for 4% of the time, Pallas kernels for 0%

commit v1 on v0

--- a/solution.py
+++ b/solution.py
@@ -1,6 +1,10 @@
+import functools
+
 import jax
 import jax.numpy as jnp
 from jax import lax
+from jax.experimental import pallas as pl
+from jax.experimental.pallas import tpu as pltpu
 from jax.sharding import PartitionSpec as P
 
 HD = 128
@@ -51,7 +55,7 @@
     return (highest, totals, accum)
 
 
-def shards(
+def gathered_weights(
     queries,
     cache_keys,
     cache_values,
@@ -111,9 +115,472 @@
     return (summed + mlp.reshape(row_count, step_count, features)).astype(jnp.bfloat16)
 
 
+MESH = pl.DeviceIdType.MESH
+BF16, F32 = jnp.bfloat16, jnp.float32
+
+
+def layer_kernel(
+    n_g,
+    n_t,
+    lengths_ref,
+    q_ref,
+    nk_ref,
+    nv_ref,
+    res_ref,
+    gain_ref,
+    ck_hbm,
+    cv_hbm,
+    wg_hbm,
+    wd_hbm,
+    mlp_ref,
+    sum_ref,
+    ck,
+    cv,
+    wg32,
+    wd32,
+    wg,
+    wd,
+    send_o,
+    recv_o,
+    send_l,
+    recv_l,
+    send_x,
+    recv_x,
+    x_rows,
+    send_g,
+    recv_g,
+    send_h,
+    recv_h,
+    send_m,
+    recv_m,
+    m_rows,
+    send_f,
+    load_sem,
+    w_sem,
+    o_send_sem,
+    o_recv_sem,
+    l_send_sem,
+    l_recv_sem,
+    c_send_sem,
+    c_recv_sem,
+    x_send_sem,
+    x_recv_sem,
+    g_send_sem,
+    g_recv_sem,
+    h_send_sem,
+    h_recv_sem,
+    m_send_sem,
+    m_recv_sem,
+    f_send_sem,
+    f_recv_sem,
+):
+    g, t = lax.axis_index("grp"), lax.axis_index("tp")
+    n = n_g * n_t
+    rows, positions = ck.shape[0], ck.shape[1]
+    steps = nk_ref.shape[1]
+    heads = gain_ref.shape[0]
+    per_key = heads // KVH
+    per_col = heads // n_g
+    inv_root = HD ** (-0.5)
+
+    def peer(k):
+        return lax.rem(g + k // n_t, n_g), lax.rem(t + lax.rem(k, n_t), n_t)
+
+    def cache_copy(r, which):
+        source, target = ((ck_hbm, ck), (cv_hbm, cv))[which]
+        return pltpu.make_async_copy(source.at[r], target.at[r], load_sem.at[which, r])
+
+    order = [lax.rem(t + k, n_t) for k in (*range(1, n_t), 0)]
+    for r in order:
+        cache_copy(r, 0).start()
+        cache_copy(r, 1).start()
+    load_gate = pltpu.make_async_copy(wg_hbm, wg32, w_sem.at[0])
+    load_down = pltpu.make_async_copy(wd_hbm, wd32, w_sem.at[1])
+    load_gate.start()
+    load_down.start()
+
+    barrier = pltpu.get_barrier_semaphore()
+
+    def greet(k, carry):
+        pl.semaphore_signal(barrier, inc=1, device_id=peer(k), device_id_type=MESH)
+        return carry
+
+    lax.fori_loop(1, n, greet, 0)
+
+    sub = lax.broadcasted_iota(jnp.int32, (steps * heads, HD), 0)
+    lane = lax.broadcasted_iota(jnp.int32, (steps * heads, HD), 1)
+    diagonal = sub == lane
+
+    row_copies = []
+    for k, r in enumerate(order):
+        cache_copy(r, 0).wait()
+        cache_copy(r, 1).wait()
+        place = t * positions + lax.broadcasted_iota(
+            jnp.int32, (steps * per_key, positions), 1
+        )
+        visible = place < lengths_ref[r]
+        query = q_ref[r].astype(F32)
+        parts, logs = [], []
+        for j in range(KVH):
+            own = jnp.concatenate(
+                [
+                    query[s * heads + j * per_key : s * heads + (j + 1) * per_key]
+                    for s in range(steps)
+                ],
+                axis=0,
+            ).astype(BF16)
+            keys = ck[r, :, j * HD : (j + 1) * HD]
+            values = cv[r, :, j * HD : (j + 1) * HD]
+            scores = (
+                lax.dot_general(own, keys, (((1,), (1,)), ((), ())), preferred_element_type=F32)
+                * inv_root
+            )
+            scores = jnp.where(visible, scores, masked_score)
+            highest = jnp.max(scores, axis=-1, keepdims=True)
+            weights = jnp.where(visible, jnp.exp(scores - highest), 0.0)
+            total = jnp.sum(weights, axis=-1, keepdims=True)
+            accum = jnp.dot(weights.astype(BF16), values, preferred_element_type=F32)
+            some = total > 0.0
+            safe = jnp.where(some, total, 1.0)
+            parts.append(accum / safe)
+            logs.append(jnp.where(some, highest + jnp.log(safe), masked_score))
+
+        def by_step(pieces):
+            return jnp.concatenate(
+                [p[s * per_key : (s + 1) * per_key] for s in range(steps) for p in pieces], axis=0
+            )
+
+        mean_values = by_step(parts).astype(BF16)
+        log_lanes = jnp.sum(
+            jnp.where(diagonal, by_step(logs), 0.0), axis=0, keepdims=True
+        )
+        log_lanes = jnp.broadcast_to(log_lanes, recv_l.shape[1:])
+        if k == n_t - 1:
+            recv_o[t] = mean_values
+            recv_l[t] = log_lanes
+        else:
+            send_o[k] = mean_values
+            send_l[k] = log_lanes
+            if k == 0:
+                pl.semaphore_wait(barrier, n - 1)
+            for source, target, send_sem, recv_sem in (
+                (send_o, recv_o, o_send_sem, o_recv_sem),
+                (send_l, recv_l, l_send_sem, l_recv_sem),
+            ):
+                copy = pltpu.make_async_remote_copy(
+                    src_ref=source.at[k],
+                    dst_ref=target.at[t],
+                    send_sem=send_sem.at[k],
+                    recv_sem=recv_sem.at[k],
+                    device_id=(g, r),
+                    device_id_type=MESH,
+                )
+                copy.start()
+                row_copies.append(copy)
+
+    query = q_ref[t].astype(F32)
+    new_keys = nk_ref[t].astype(F32)
+    new_values = nv_ref[t].astype(F32)
+
+    def over_heads(tokens, at):
+        return jnp.concatenate(
+            [
+                jnp.broadcast_to(tokens[at : at + 1, j * HD : (j + 1) * HD], (per_key, HD))
+                for _ in range(steps)
+                for j in range(KVH)
+            ],
+            axis=0,
+        )
+
+    seen = [
+        lax.broadcasted_iota(jnp.int32, (steps * heads, 1), 0) >= at * heads for at in range(steps)
+    ]
+    fresh = [
+        jnp.where(
+            seen[at],
+            jnp.sum(query * over_heads(new_keys, at), axis=-1, keepdims=True) * inv_root,
+            masked_score,
+        )
+        for at in range(steps)
+    ]
+    load_gate.wait()
+    wg[...] = wg32[...].astype(BF16)
+    load_down.wait()
+    wd[...] = wd32[...].astype(BF16)
+    for copy in row_copies:
+        copy.wait_recv()
+
+    logs = [
+        jnp.sum(jnp.where(diagonal, recv_l[i][0:1], 0.0), axis=-1, keepdims=True)
+        for i in range(n_t)
+    ]
+    joint = functools.reduce(jnp.maximum, logs + fresh)
+    total, accum = 0.0, 0.0
+    for i in range(n_t):
+        weight = jnp.exp(logs[i] - joint)
+        total = total + weight
+        accum = accum + weight * recv_o[i].astype(F32)
+    for at in range(steps):
+        weight = jnp.where(seen[at], jnp.exp(fresh[at] - joint), 0.0)
+        total = total + weight
+        accum = accum + weight.astype(BF16).astype(F32) * over_heads(new_values, at)
+    summed = res_ref[t].astype(F32) + accum / total
+
+    normed = []
+    for s in range(steps):
+        part = summed[s * heads : (s + 1) * heads]
+        square = jnp.sum(jnp.sum(part * part, axis=0, keepdims=True), axis=1, keepdims=True)
+        normed.append(part * lax.rsqrt(square / (heads * HD) + 1e-05) * gain_ref[...])
+    for i in range(n_g):
+        send_x[i] = jnp.concatenate(
+            [part[i * per_col : (i + 1) * per_col] for part in normed], axis=0
+        ).astype(BF16)
+
+    def to_all(source, target, send_sem, recv_sem):
+        def one(k):
+            to_g, to_t = peer(k)
+            return pltpu.make_async_remote_copy(
+                src_ref=source.at[to_g],
+                dst_ref=target.at[t * n_g + g],
+                send_sem=send_sem.at[k - 1],
+                recv_sem=recv_sem.at[k - 1],
+                device_id=(to_g, to_t),
+                device_id_type=MESH,
+            )
+
+        return one
+
+    def start_all(one):
+        def body(k, carry):
+            one(k).start()
+            return carry
+
+        lax.fori_loop(1, n, body, 0)
+
+    def wait_all(one, sent):
+        def body(k, carry):
+            if sent:
+                one(k).wait_send()
+            else:
+                one(k).wait_recv()
+            return carry
+
+        lax.fori_loop(1, n, body, 0)
+
+    x_copy = to_all(send_x, recv_x, x_send_sem, x_recv_sem)
+    start_all(x_copy)
+    recv_x[t * n_g + g] = send_x[g]
+    sum_ref[t] = summed.astype(BF16)
+    sum_copies = []
+    for k in range(1, n_t):
+        copy = pltpu.make_async_remote_copy(
+            src_ref=sum_ref.at[t],
+            dst_ref=sum_ref.at[t],
+            send_sem=c_send_sem.at[k - 1],
+            recv_sem=c_recv_sem.at[k - 1],
+            device_id=(g, lax.rem(t + k, n_t)),
+            device_id_type=MESH,
+        )
+        copy.start()
+        sum_copies.append(copy)
+    wait_all(x_copy, False)
+
+    height = steps * per_col
+    x_rows[...] = recv_x[...].astype(F32).reshape(n * height, HD)
+    columns = []
+    for c in range(per_col):
+        picked = [x_rows[pl.ds(s * per_col + c, n, stride=height), :] for s in range(steps)]
+        columns.append(
+            jnp.concatenate(
+                [p[i * n_g : (i + 1) * n_g] for i in range(n_t) for p in picked], axis=0
+            )
+        )
+    x = jnp.concatenate(columns, axis=1).astype(BF16)
+    gate = jnp.dot(x, wg[...], preferred_element_type=F32)
+    chunk = send_g.shape[1]
+    for i in range(n_g):
+        send_g[i] = gate[i * chunk : (i + 1) * chunk].astype(BF16)
+
+    def along_grp(k, source, target, send_sem, recv_sem):
+        return pltpu.make_async_remote_copy(
+            src_ref=source,
+            dst_ref=target.at[g],
+            send_sem=send_sem.at[k - 1],
+            recv_sem=recv_sem.at[k - 1],
+            device_id=(lax.rem(g + k, n_g), t),
+            device_id_type=MESH,
+        )
+
+    gate_copies = [
+        along_grp(k, send_g.at[lax.rem(g + k, n_g)], recv_g, g_send_sem, g_recv_sem)
+        for k in range(1, n_g)
+    ]
+    for copy in gate_copies:
+        copy.start()
+    recv_g[g] = send_g[g]
+    for copy in gate_copies:
+        copy.wait_recv()
+    whole = functools.reduce(jnp.add, [recv_g[i].astype(F32) for i in range(n_g)])
+    mine = (whole / (1.0 + jnp.exp(-whole))).astype(BF16)
+
+    send_h[...] = mine
+    hidden_copies = [
+        along_grp(k, send_h, recv_h, h_send_sem, h_recv_sem) for k in range(1, n_g)
+    ]
+    for copy in hidden_copies:
+        copy.start()
+    recv_h[g] = mine
+    for copy in hidden_copies:
+        copy.wait_recv()
+    hidden = recv_h[...].astype(F32).reshape(n_g * chunk, recv_h.shape[2]).astype(BF16)
+    mlp = lax.dot_general(hidden, wd[...], (((1,), (1,)), ((), ())), preferred_element_type=F32)
+
+    part_rows = send_m.shape[1]
+    for i in range(n_t):
+        send_m[i] = mlp[i * part_rows : (i + 1) * part_rows].astype(BF16)
+    mlp_copies = []
+    for k in range(1, n_t):
+        to_t = lax.rem(t + k, n_t)
+        copy = pltpu.make_async_remote_copy(
+            src_ref=send_m.at[to_t],
+            dst_ref=recv_m.at[t],
+            send_sem=m_send_sem.at[k - 1],
+            recv_sem=m_recv_sem.at[k - 1],
+            device_id=(g, to_t),
+            device_id_type=MESH,
+        )
+        copy.start()
+        mlp_copies.append(copy)
+    recv_m[t] = send_m[t]
+    for copy in mlp_copies:
+        copy.wait_recv()
+    done = functools.reduce(jnp.add, [recv_m[i].astype(F32) for i in range(n_t)])
+
+    for s in range(steps):
+        for c in range(per_col):
+            m_rows[pl.ds(s * per_col + c, n_g, stride=height), :] = done[
+                s * n_g : (s + 1) * n_g, c * HD : (c + 1) * HD
+            ]
+    send_f[...] = m_rows[...].reshape(n_g, height, HD).astype(BF16)
+    f_copy = to_all(send_f, mlp_ref, f_send_sem, f_recv_sem)
+    start_all(f_copy)
+    mlp_ref[t * n_g + g] = send_f[g]
+    for copy in row_copies + sum_copies + gate_copies + hidden_copies + mlp_copies:
+        copy.wait_send()
+    wait_all(x_copy, True)
+    for copy in sum_copies:
+        copy.wait_recv()
+    wait_all(f_copy, False)
+    wait_all(f_copy, True)
+
+
+def moved_activations(
+    n_g,
+    n_t,
+    queries,
+    cache_keys,
+    cache_values,
+    new_keys,
+    new_values,
+    lengths,
+    residual,
+    norm_gain,
+    w_gate,
+    w_down,
+):
+    rows, steps, features = queries.shape
+    positions, kv_width = cache_keys.shape[1:]
+    depth, units = w_gate.shape
+    heads = features // HD
+    n = n_g * n_t
+    flat = steps * heads
+    height = steps * (heads // n_g)
+    all_rows = n * steps
+    chunk = all_rows // n_g
+    part_rows = all_rows // n_t
+    vmem = pl.BlockSpec(memory_space=pltpu.VMEM)
+    hbm = pl.BlockSpec(memory_space=pl.ANY)
+    dma = pltpu.SemaphoreType.DMA
+    mlp, summed = pl.pallas_call(
+        functools.partial(layer_kernel, n_g, n_t),
+        out_shape=(
+            jax.ShapeDtypeStruct((n, height, HD), BF16),
+            jax.ShapeDtypeStruct((n_t, flat, HD), BF16),
+        ),
+        in_specs=[pl.BlockSpec(memory_space=pltpu.SMEM)] + [vmem] * 5 + [hbm] * 4,
+        out_specs=(vmem, vmem),
+        scratch_shapes=[
+            pltpu.VMEM((rows, positions, kv_width), BF16),
+            pltpu.VMEM((rows, positions, kv_width), BF16),
+            pltpu.VMEM((depth, units), F32),
+            pltpu.VMEM((depth, units), F32),
+            pltpu.VMEM((depth, units), BF16),
+            pltpu.VMEM((depth, units), BF16),
+            pltpu.VMEM((n_t, flat, HD), BF16),
+            pltpu.VMEM((n_t, flat, HD), BF16),
+            pltpu.VMEM((n_t, 8, HD), F32),
+            pltpu.VMEM((n_t, 8, HD), F32),
+            pltpu.VMEM((n_g, height, HD), BF16),
+            pltpu.VMEM((n, height, HD), BF16),
+            pltpu.VMEM((n * height, HD), F32),
+            pltpu.VMEM((n_g, chunk, units), BF16),
+            pltpu.VMEM((n_g, chunk, units), BF16),
+            pltpu.VMEM((chunk, units), BF16),
+            pltpu.VMEM((n_g, chunk, units), BF16),
+            pltpu.VMEM((n_t, part_rows, depth), BF16),
+            pltpu.VMEM((n_t, part_rows, depth), BF16),
+            pltpu.VMEM((n_g * height, HD), F32),
+            pltpu.VMEM((n_g, height, HD), BF16),
+            dma((2, rows)),
+            dma((2,)),
+        ]
+        + [dma((n_t,))] * 6
+        + [dma((n,))] * 2
+        + [dma((n_g,))] * 4
+        + [dma((n_t,))] * 2
+        + [dma((n,))] * 2,
+        compiler_params=pltpu.CompilerParams(
+            collective_id=0, has_side_effects=True, vmem_limit_bytes=32 * 1024 * 1024
+        ),
+    )(
+        lengths,
+        queries.reshape(rows, flat, HD),
+        new_keys,
+        new_values,
+        residual.reshape(rows, flat, HD),
+        norm_gain.reshape(heads, HD),
+        cache_keys,
+        cache_values,
+        w_gate,
+        w_down,
+    )
+    mlp = mlp.reshape(n_t, n_g, steps, heads // n_g, HD).transpose(0, 2, 1, 3, 4)
+    total = summed.reshape(rows, steps, features).astype(F32) + mlp.reshape(
+        rows, steps, features
+    ).astype(F32)
+    return total.astype(BF16)
+
+
+def shards(n_g, n_t, *arrays):
+    queries = arrays[0]
+    rows, steps, features = queries.shape
+    heads = features // HD
+    even = (
+        rows == n_t
+        and heads % n_g == 0
+        and n_g % 8 == 0
+        and steps * (heads // n_g) == 8
+        and steps * heads <= HD
+        and (steps * n_t) % 8 == 0
+    )
+    if even:
+        return moved_activations(n_g, n_t, *arrays)
+    return gathered_weights(*arrays)
+
+
 def solution(mesh):
     return jax.shard_map(
-        shards,
+        functools.partial(shards, mesh.shape["grp"], mesh.shape["tp"]),
         mesh=mesh,
         in_specs=(
             P("grp", None, None),

time: 145 us -> 45.5 us (0.31)
  waiting for transfers between devices: 72.6 us -> 0 us
  blocking collectives: 41.7 us -> 0 us
  Pallas kernels: 0 us -> 37.9 us
  between operations: 13.4 us -> 0.15 us
  matrix products: 7.78 us -> 0 us
  other arithmetic: 7.49 us -> 0.71 us
  local copies, waits for them, and re-layouts: 1.21 us -> 6.48 us
    all_gather x3 -> x0, blocking collectives: 41.7 us -> none  [merged_2(): lax.all_gather(a.astype(kind), axis)]
    all_gather x2 -> x0, waiting for transfers between devices: 38.4 us -> none  [the longest x1 38.4 us: shards(): lax.all_gather(w_down.astype(jnp.bfloat16), 'grp', axis=0, tiled=True)]
    pallas_call x0 -> x1, Pallas kernels: none -> 37.9 us  [moved_activations(): pl.pallas_call(functools.partial(layer_kernel, n_g, n_t), out_shape=(jax....]
    psum x1 -> x0, waiting for transfers between devices: 34.1 us -> none  [shards(): mlp = lax.psum(partial_sum.astype(jnp.bfloat16), 'tp').astype(jnp.float32)]
    dot_general x5 -> x0, matrix products: 7.78 us -> none  [the longest x1 6.29 us: shards(): lax.dot_general(hidden, down_policy, (((1,), (1,)), ((), ())), preferred_...]
    convert_element_type x8 -> x1, other arithmetic: 6.25 us -> 0.7 us  [moved_activations(): return total.astype(BF16)]
    unnamed x16 -> x14, local copies, waits for them, and re-layouts: 0.03 us -> 4.49 us
  transfers between devices with their start and end apart: 3 -> 0, of which waited for: 2 -> 0; matrix products, arithmetic and copies ran while one was open for 4% -> 0% of each run, Pallas kernels for 0% -> 0%
where the time goes in v1:
time: 45.5 us; the launch traced here: 45.2 us
  Pallas kernels  37.9 us (83%)
  local copies, waits for them, and re-layouts  6.48 us (14%)
  other arithmetic  0.71 us (2%)
    pallas_call x1, Pallas kernels, moved_activations(): pl.pallas_call(functools.partial(layer_kernel, n_g, n_t), out_shape=(jax....  37.9 us
    unnamed x14, local copies, waits for them, and re-layouts  4.49 us

profile of v1, /device:TPU:0, one launch (start us, length us, event | category | flops | bytes accessed | tf_op | source)
XLA Modules:
  0.0 45.2 jit_solution(16991978868789155896)
XLA Ops:
  0.0 0.9 %reshape.18.q_ref = bf16[4,64,128]{2,1,0:T(8,128)(2,1)S(1)} reshape(bf16[4,2,4096]{2,1,0:T(2,128)(2,1)} %param.10) | data formatting | bytes 131072 | tf_op jit(solution)/shard_map/reshape | solution.py:547
  0.9 0.9 %reshape.19.res_ref = bf16[4,64,128]{2,1,0:T(8,128)(2,1)S(1)} reshape(bf16[4,2,4096]{2,1,0:T(2,128)(2,1)} %param.16) | data formatting | bytes 131072 | tf_op jit(solution)/shard_map/reshape | solution.py:550
  1.8 1.7 %copy.11.wg_hbm = f32[512,600]{1,0:T(8,128)S(1)} copy(f32[512,600]{0,1:T(8,128)} %param.18) | data formatting | bytes 2457600 | tf_op args[8]
  3.5 0.0 copy-start
  3.5 0.0 copy-start.2
  3.5 0.0 copy-start.3
  3.5 0.0 copy-start.4
  3.5 0.0 copy-start.5
  3.6 1.7 %copy.12.wd_hbm = f32[512,600]{1,0:T(8,128)S(1)} copy(f32[512,600]{0,1:T(8,128)} %param.19) | data formatting | bytes 2457600 | tf_op args[9]
  5.3 0.0 copy-done
  5.3 0.0 copy-done.2
  5.3 0.0 copy-done.3
  5.3 0.0 copy-done.4
  5.3 0.0 copy-done.5
  5.3 0.0 copy-start.1
  5.4 1.0 %copy-done.1 = bf16[4,128,512]{2,1,0:T(8,128)(2,1)S(1)} copy-done((bf16[4,128,512]{2,1,0:T(8,128)(2,1)S(1)}, bf16[4,128,512]{2,1,0:T(8,128)(2,1)}, u32[]{:S(2)}) %copy-start.1) | copy-done | bytes 524312
  6.4 37.9 %shard_map.100 = (bf16[32,8,128]{2,1,0:T(8,128)(2,1)S(1)}, bf16[4,64,128]{2,1,0:T(8,128)(2,1)S(1)}) custom-call(s32[4]{0:T(128)S(1)} %copy-done.5, bf16[4,64,128]{2,1,0:T(8,128)(2,1)S(1)} %reshape.18.q_ref, bf16[4,2,512]{2,1,0:T(2,128)(2,1)S(1)} %copy-done.3, bf16[4,2,512]{2,1,0:T(2,128)(2,1)S(1)} %copy-done.4, bf16[4,64,128]{2,1,0:T(8,128)(2,1)S(1)} %reshape.19.res_ref, ...), custom_call_target="tpu_custom_call" | custom-call | tf_op jit(solution)/shard_map/pallas_call | solution.py:504
  44.3 0.1 reshape.21
  44.4 0.1 reshape.22
  44.5 0.7 %add_convert_fusion = bf16[4,2,4096]{2,1,0:T(2,128)(2,1)} fusion(f32[4,2,4096]{2,1,0:T(2,128)S(1)} %reshape.21, f32[4,2,4096]{2,1,0:T(2,128)S(1)} %reshape.22), kind=kLoop, calls=%fused_computation | loop fusion | flops 65536 | bytes 327680 | tf_op jit(solution)/shard_map/convert_element_type | solution.py:561
  (2 shorter events, 0.0 us)
Async XLA Ops:
  3.5 1.8 %copy-start = (bf16[4,128,512]{2,1,0:T(8,128)(2,1)S(1)}, bf16[4,128,512]{2,1,0:T(8,128)(2,1)}, u32[]{:S(2)}) copy-start(bf16[4,128,512]{2,1,0:T(8,128)(2,1)} %ck_hbm.1) | copy-start | bytes 1572868
  3.5 1.8 %copy-start.2 = (f32[4096]{0:T(1024)S(1)}, f32[4096]{0:T(1024)}, u32[]{:S(2)}) copy-start(f32[4096]{0:T(1024)} %param.17) | copy-start | bytes 49156
  3.5 1.8 %copy-start.3 = (bf16[4,2,512]{2,1,0:T(2,128)(2,1)S(1)}, bf16[4,2,512]{2,1,0:T(2,128)(2,1)}, u32[]{:S(2)}) copy-start(bf16[4,2,512]{2,1,0:T(2,128)(2,1)} %nk_ref.1) | copy-start | bytes 24580
  3.5 1.8 %copy-start.4 = (bf16[4,2,512]{2,1,0:T(2,128)(2,1)S(1)}, bf16[4,2,512]{2,1,0:T(2,128)(2,1)}, u32[]{:S(2)}) copy-start(bf16[4,2,512]{2,1,0:T(2,128)(2,1)} %nv_ref.1) | copy-start | bytes 24580
  3.5 1.8 %copy-start.5 = (s32[4]{0:T(128)S(1)}, s32[4]{0:T(128)}, u32[]{:S(2)}) copy-start(s32[4]{0:T(128)} %lengths_ref.1) | copy-start | bytes 52
  5.3 1.0 %copy-start.1 = (bf16[4,128,512]{2,1,0:T(8,128)(2,1)S(1)}, bf16[4,128,512]{2,1,0:T(8,128)(2,1)}, u32[]{:S(2)}) copy-start(bf16[4,128,512]{2,1,0:T(8,128)(2,1)} %cv_hbm.1) | copy-start | bytes 1572868
